TPU v7x, 512 devices: a whole 4x4x16 slice. The times are simulated.
512 devices in a mesh: expert: 128 (over y, z, core), half: 4 (over x).
Axes of the slice: x: 4, y: 4, z: 16, core: 2. Of those that a mesh axis runs over, the one named last changes fastest.
Arguments:
- tokens: bfloat16 [2048, 2048], P('expert', 'half'), may hold values from -6 to 6
- upstream: bfloat16 [2048, 2048], P('expert', 'half'), may hold values from -6 to 6
- expert_ids: int32 [2048, 8], P('expert'), may hold values from 0 to 127, all different within a row; in each aligned block of 16 rows (0 to 15, 16 to 31, ...) at most 2 rows name the same one
- gate_probs: float32 [2048, 8], P('expert'), may hold values from 0.01 to 1
- pad_mask: int32 [2048], P('expert'), may hold values 0 or 1
- gate_weight: bfloat16 [128, 2048, 1536], P('expert', None, 'half'), may hold values from -0.125 to 0.125
- up_weight: bfloat16 [128, 2048, 1536], P('expert', None, 'half'), may hold values from -0.125 to 0.125
- down_weight: bfloat16 [128, 1536, 2048], P('expert', 'half'), may hold values from -0.15625 to 0.15625
Outputs:
- layer_out: bfloat16 [2048, 2048], P('expert', 'half')
- grad_tokens: bfloat16 [2048, 2048], P('expert', 'half')
Inputs may be any that keep to these rules, and one draw needn't show every extreme that they name: `expert_ids`: each row names 8 different experts. In the rows of one device (aligned blocks of 16 rows) no expert is named more than 2 times, a bound that some block reaches.
All inputs are finite; a program needn't handle non-finite values. No bound on the sum of `pad_mask` on one device may be relied on, other than what follows from the above.
Results may differ from a plain program's by a relative error of at most 0.025.
Values may be sent and summed in bfloat16 or wider, within the bound.
No kernel may reach another device: no remote copies, remote signals or barrier semaphores. Data moves between devices by JAX's collectives and lax.ppermute only.
A program may use at most 64 MiB of HBM per device.

v0:
```python
import math
import jax
import jax.numpy as jnp
from jax import lax
from jax.sharding import PartitionSpec as P

orth_weight = 0.25


def assign_slots(expert_ids, experts, capacity):
    tok_count, top_count = expert_ids.shape
    flat_ids = expert_ids.reshape(tok_count * top_count)
    onehot = (flat_ids[:, None] == jnp.arange(experts, dtype=jnp.int32)[None, :]).astype(jnp.int32)
    before = jnp.cumsum(onehot, axis=0) - onehot
    slot_index = jnp.sum(before * onehot, axis=1)
    return flat_ids * capacity + slot_index


def placement_matrix(slot_dest, slots_total):
    row_index = jnp.arange(slots_total, dtype=jnp.int32)
    return (row_index[:, None] == slot_dest[None, :]).astype(jnp.bfloat16)


def to_experts(place, items):
    whole = lax.all_gather(items, "half", axis=1, tiled=True)
    buckets = jnp.dot(place, whole, preferred_element_type=jnp.float32).astype(jnp.bfloat16)
    return lax.all_to_all(buckets, "expert", split_axis=0, concat_axis=0, tiled=True)


def to_homes(partial_value):
    summed = lax.psum_scatter(
        partial_value.astype(jnp.bfloat16), "half", scatter_dimension=1, tiled=True
    )
    return lax.all_to_all(summed, "expert", split_axis=0, concat_axis=0, tiled=True)


def shards(tokens, upstream, expert_ids, gate_probs, pad_mask, gate_weight, up_weight, down_weight):
    tok_count, top_count = expert_ids.shape
    experts = lax.axis_size("expert")
    capacity = min(tok_count, 2 * tok_count * top_count // experts)
    slots_total = experts * capacity
    full_width = tokens.shape[1] * lax.axis_size("half")
    slot_dest = assign_slots(expert_ids, experts, capacity)
    place_items = placement_matrix(slot_dest, slots_total)
    place_tokens = jnp.sum(place_items.reshape(slots_total, tok_count, top_count), axis=2)
    weight_gate = gate_weight[0]
    weight_up = up_weight[0]
    weight_down = down_weight[0]
    rows_in = to_experts(place_tokens, tokens)
    gate_val = jnp.dot(rows_in, weight_gate, preferred_element_type=jnp.float32)
    up_val = jnp.dot(rows_in, weight_up, preferred_element_type=jnp.float32)
    hidden_act = (jax.nn.silu(gate_val) * up_val).astype(jnp.bfloat16)
    partial_value = jnp.dot(hidden_act, weight_down, preferred_element_type=jnp.float32)
    out_home = to_homes(partial_value)
    outputs = jnp.take(out_home, slot_dest, axis=0).reshape(tok_count, top_count, -1)
    out_float = outputs.astype(jnp.float32)
    shares = gate_probs / jnp.sum(gate_probs, axis=1, keepdims=True)
    layer_out = jnp.sum(shares[:, :, None] * out_float, axis=1).astype(jnp.bfloat16)
    gram_part = jnp.einsum("tjd,tkd->tjk", out_float, out_float) / math.sqrt(full_width)
    gram = lax.psum(gram_part, "half")
    off_diag = 1.0 - jnp.eye(top_count, dtype=jnp.float32)
    coeffs = orth_weight * gram * off_diag
    grad_out = pad_mask.astype(jnp.float32)[:, None, None] * (
        shares[:, :, None] * upstream.astype(jnp.float32)[:, None, :]
        + jnp.einsum("tjk,tkd->tjd", coeffs, out_float)
    )
    grad_items = grad_out.astype(jnp.bfloat16).reshape(tok_count * top_count, -1)
    grad_rows = to_experts(place_items, grad_items)
    grad_act = jnp.einsum("rd,hd->rh", grad_rows, weight_down, preferred_element_type=jnp.float32)
    sigma = jax.nn.sigmoid(gate_val)
    grad_gate = (grad_act * up_val * sigma * (1.0 + gate_val * (1.0 - sigma))).astype(jnp.bfloat16)
    grad_up = (grad_act * gate_val * sigma).astype(jnp.bfloat16)
    grad_partial = jnp.einsum(
        "rh,dh->rd", grad_gate, weight_gate, preferred_element_type=jnp.float32
    )
    grad_partial = grad_partial + jnp.einsum(
        "rh,dh->rd", grad_up, weight_up, preferred_element_type=jnp.float32
    )
    grad_home = to_homes(grad_partial)
    grad_pairs = jnp.take(grad_home, slot_dest, axis=0).reshape(tok_count, top_count, -1)
    grad_tokens = jnp.sum(grad_pairs.astype(jnp.float32), axis=1).astype(jnp.bfloat16)
    return (layer_out, grad_tokens)


def solution(mesh):
    in_specs = (
        P("expert", "half"),
        P("expert", "half"),
        P("expert", None),
        P("expert", None),
        P("expert"),
        P("expert", None, "half"),
        P("expert", None, "half"),
        P("expert", "half", None),
    )
    out_specs = (P("expert", "half"), P("expert", "half"))
    return jax.shard_map(shards, mesh=mesh, in_specs=in_specs, out_specs=out_specs, check_vma=False)
```

profile of v0, /device:TPU:1, one launch (start us, length us, event | category | flops | bytes accessed | tf_op | source)
XLA Modules:
  0.0 342.9 jit_solution(6629864669466501402)
XLA Ops:
  7.2 0.9 copy.17
  8.9 10.4 %all_gather.6 = bf16[16,2048]{1,0:T(8,128)(2,1)S(1)} all-gather(bf16[16,512]{1,0:T(8,128)(2,1)} %param.10), channel_id=1, replica_groups=mesh['expert'=128,'half'=4] {'half'}, dimensions={1}, use_global_device_ids=true | all-gather | bytes 81920 | tf_op jit(solution)/shard_map/all_gather | solution.py:25
  19.2 0.5 convolution_convert_fusion.2
  19.7 1.5 all_to_all.32
  21.2 77.1 %all_to_all.48 = bf16[128,2,2048]{2,1,0:T(2,128)(2,1)} all-to-all(bf16[128,2,2048]{2,1,0:T(2,128)(2,1)} %all_to_all.32), channel_id=1, replica_groups=mesh['expert'=128,'half'=4] {'expert'}, dimensions={0} | all-to-all | bytes 2097152 | tf_op jit(solution)/shard_map/all_to_all | solution.py:27
  98.3 1.5 all_to_all.34
  99.8 2.2 fusion.9
  102.0 0.7 fusion.5
  102.7 1.7 convolution_convert_fusion.1
  104.5 22.2 %reduce-scatter.3.cloned.1.call-done = bf16[256,512]{1,0:T(8,128)(2,1)} async-done(((bf16[256,2048]{1,0:T(8,128)(2,1)}), bf16[256,512]{1,0:T(8,128)(2,1)}) %reduce-scatter.3.cloned.1.call-update) | async-done | bytes 262160 | tf_op jit(solution)/shard_map/reduce_scatter | solution.py:31
  126.7 1.7 all_to_all.35
  128.4 18.4 %all-to-all-start.1 = ((bf16[128,2,512]{2,1,0:T(2,128)(2,1)}), bf16[128,2,512]{2,1,0:T(2,128)(2,1)S(1)}, u32[]{:S(2)}, u32[]{:S(2)}) async-start(bf16[128,2,512]{2,1,0:T(2,128)(2,1)} %all_to_all.35), calls=%async_computation.2 | async-start | bytes 524288 | tf_op jit(solution)/shard_map/all_to_all | solution.py:34
  147.1 22.2 %all-to-all-done.1 = bf16[128,2,512]{2,1,0:T(2,128)(2,1)S(1)} async-done(((bf16[128,2,512]{2,1,0:T(2,128)(2,1)}), bf16[128,2,512]{2,1,0:T(2,128)(2,1)S(1)}, u32[]{:S(2)}, u32[]{:S(2)}) %all-to-all-start.1) | async-done | bytes 262176 | tf_op jit(solution)/shard_map/all_to_all | solution.py:34
  169.4 0.8 gather_fusion
  170.5 11.8 %psum.7 = f32[16,8,8]{2,1,0:T(8,128)S(1)} all-reduce(f32[16,8,8]{2,1,0:T(8,128)S(1)} %convolution_multiply_fusion), channel_id=1, replica_groups=mesh['expert'=128,'half'=4] {'half'}, use_global_device_ids=true, to_apply=%region_6.8 | all-reduce | flops 1024 | bytes 8192 | tf_op jit(solution)/shard_map/psum | solution.py:60
  182.6 10.1 %all_gather.7 = bf16[128,2048]{1,0:T(8,128)(2,1)S(1)} all-gather(bf16[128,512]{1,0:T(8,128)(2,1)S(1)} %fusion.13), channel_id=1, replica_groups=mesh['expert'=128,'half'=4] {'half'}, dimensions={1}, use_global_device_ids=true | all-gather | bytes 655360 | tf_op jit(solution)/shard_map/all_gather | solution.py:25
  192.7 1.1 convolution_convert_fusion
  193.8 1.5 all_to_all.38
  195.3 69.1 %all_to_all.49 = bf16[128,2,2048]{2,1,0:T(2,128)(2,1)} all-to-all(bf16[128,2,2048]{2,1,0:T(2,128)(2,1)} %all_to_all.38), channel_id=1, replica_groups=mesh['expert'=128,'half'=4] {'expert'}, dimensions={0} | all-to-all | bytes 2097152 | tf_op jit(solution)/shard_map/all_to_all | solution.py:27
  264.4 1.5 all_to_all.40
  265.9 0.7 fusion.1
  266.6 0.7 copy-done.1
  267.3 0.8 fusion.7
  268.1 0.6 copy-done.3
  268.7 1.8 fusion
  270.5 20.9 %reduce-scatter.5.cloned.1.call-done = bf16[256,512]{1,0:T(8,128)(2,1)} async-done(((bf16[256,2048]{1,0:T(8,128)(2,1)}), bf16[256,512]{1,0:T(8,128)(2,1)}) %reduce-scatter.5.cloned.1.call-update) | async-done | bytes 262160 | tf_op jit(solution)/shard_map/reduce_scatter | solution.py:31
  291.4 1.7 all_to_all.41
  293.2 18.7 %all-to-all-start.3 = ((bf16[128,2,512]{2,1,0:T(2,128)(2,1)}), bf16[128,2,512]{2,1,0:T(2,128)(2,1)S(1)}, u32[]{:S(2)}, u32[]{:S(2)}) async-start(bf16[128,2,512]{2,1,0:T(2,128)(2,1)} %all_to_all.41), calls=%async_computation.5 | async-start | bytes 524288 | tf_op jit(solution)/shard_map/all_to_all | solution.py:34
  311.9 0.8 multiply_reduce_fusion
  312.6 21.7 %all-to-all-done.3 = bf16[128,2,512]{2,1,0:T(2,128)(2,1)S(1)} async-done(((bf16[128,2,512]{2,1,0:T(2,128)(2,1)}), bf16[128,2,512]{2,1,0:T(2,128)(2,1)S(1)}, u32[]{:S(2)}, u32[]{:S(2)}) %all-to-all-start.3) | async-done | bytes 262176 | tf_op jit(solution)/shard_map/all_to_all | solution.py:34
  334.5 0.8 gather_fusion.1
  335.3 0.7 bitcast_reduce_fusion
  (38 shorter events, 1.7 us)
Async XLA Ops:
  7.2 95.6 %copy-start = (bf16[1,384,2048]{2,1,0:T(8,128)(2,1)S(1)}, bf16[1,384,2048]{2,1,0:T(8,128)(2,1)}, u32[]{:S(2)}) copy-start(bf16[1,384,2048]{2,1,0:T(8,128)(2,1)} %param.17) | copy-start | bytes 4718596
  7.2 119.5 %reduce-scatter.3.cloned.1.call-start = ((), (), s32[]{:S(2)}) async-start(), calls=%async_computation.6 | async-start | bytes 1310720 | tf_op jit(solution)/shard_map/reduce_scatter | solution.py:31
  99.8 2.2 copy-start.2
  104.5 42.4 %copy-start.7 = (s32[16]{0:T(128)S(1)}, s32[16]{0:T(128)}, u32[]{:S(2)}) copy-start(s32[16]{0:T(128)} %param.14) | copy-start | bytes 196
  104.5 42.4 %copy-start.5 = (f32[16,8]{0,1:T(8,128)S(1)}, f32[16,8]{0,1:T(8,128)}, u32[]{:S(2)}) copy-start(f32[16,8]{0,1:T(8,128)} %param.13) | copy-start | bytes 1540
  104.5 42.5 %copy-start.4 = (bf16[16,512]{1,0:T(8,128)(2,1)S(1)}, bf16[16,512]{1,0:T(8,128)(2,1)}, u32[]{:S(2)}) copy-start(bf16[16,512]{1,0:T(8,128)(2,1)} %param.11) | copy-start | bytes 49156
  128.4 40.9 %all-to-all-start.1 = ((bf16[128,2,512]{2,1,0:T(2,128)(2,1)}), bf16[128,2,512]{2,1,0:T(2,128)(2,1)S(1)}, u32[]{:S(2)}, u32[]{:S(2)}) async-start(bf16[128,2,512]{2,1,0:T(2,128)(2,1)} %all_to_all.35), calls=%async_computation.2 | async-start | bytes 524288 | tf_op jit(solution)/shard_map/all_to_all | solution.py:34
  146.8 144.6 %reduce-scatter.5.cloned.1.call-start = ((), (), s32[]{:S(2)}) async-start(), calls=%async_computation.7 | async-start | bytes 1310720 | tf_op jit(solution)/shard_map/reduce_scatter | solution.py:31
  147.0 22.3 %copy-start.6 = (s32[128]{0:T(128)}, s32[128]{0:T(128)S(1)}, u32[]{:S(2)}) copy-start(s32[128]{0:T(128)S(1)} %get-tuple-element.4) | copy-start | bytes 1540
  265.9 1.4 copy-start.1
  267.3 1.4 copy-start.3
  293.2 41.2 %all-to-all-start.3 = ((bf16[128,2,512]{2,1,0:T(2,128)(2,1)}), bf16[128,2,512]{2,1,0:T(2,128)(2,1)S(1)}, u32[]{:S(2)}, u32[]{:S(2)}) async-start(bf16[128,2,512]{2,1,0:T(2,128)(2,1)} %all_to_all.41), calls=%async_computation.5 | async-start | bytes 524288 | tf_op jit(solution)/shard_map/all_to_all | solution.py:34
Sparse Core Ops, SparseCore 0:
  104.6 22.0 reduce-scatter.2
  270.6 20.7 reduce-scatter.4
where the time goes:
time: 344 us; the launch traced here: 343 us
  blocking collectives  178 us (52%)
  waiting for transfers between devices  87.1 us (25%)
  starting transfers between devices  37.2 us (11%)
  between operations  14.3 us (4%)
  local copies, waits for them, and re-layouts  13.8 us (4%)
  matrix products  9.94 us (3%)
    all_to_all x2, blocking collectives, to_experts(): lax.all_to_all(buckets, 'expert', split_axis=0, concat_axis=0, tiled=True)  146 us
    all_to_all x2, waiting for transfers between devices, to_homes(): lax.all_to_all(summed, 'expert', split_axis=0, concat_axis=0, tiled=True)  44 us
    reduce_scatter x2, waiting for transfers between devices, to_homes(): lax.psum_scatter(partial_value.astype(jnp.bfloat16), 'half', scatter_dime...  43.1 us
    all_to_all x2, starting transfers between devices, to_homes(): lax.all_to_all(summed, 'expert', split_axis=0, concat_axis=0, tiled=True)  37.1 us
    all_gather x2, blocking collectives, to_experts(): whole = lax.all_gather(items, 'half', axis=1, tiled=True)  20.5 us
    psum x1, blocking collectives, shards(): gram = lax.psum(gram_part, 'half')  11.8 us
  transfers between devices with their start and end apart: 4, of which 4 were waited for; matrix products, arithmetic and copies ran while one was open for 0% of the time, Pallas kernels for 0%

commit v1 on v0

--- a/solution.py
+++ b/solution.py
@@ -1,10 +1,34 @@
+import functools
 import math
 import jax
 import jax.numpy as jnp
 from jax import lax
 from jax.sharding import PartitionSpec as P
+from jax.lax import axis_size, ppermute
 
 orth_weight = 0.25
+
+
+def _use_bands(values, net_axis):
+    n_blocks = axis_size(net_axis)
+
+    def perform_slot(main, part_now):
+        if part_now >= n_blocks:
+            return main
+        return perform_slot(
+            main
+            + ppermute(
+                main,
+                axis_name=net_axis,
+                perm=list(map(lambda no: (no, no ^ part_now), range(n_blocks))),
+            ),
+            2 * part_now,
+        )
+
+    return perform_slot(values, 1)
+
+
+take_quarters_here = functools.partial(_use_bands, net_axis="half")
 
 
 def assign_slots(expert_ids, experts, capacity):
@@ -57,7 +81,7 @@
     shares = gate_probs / jnp.sum(gate_probs, axis=1, keepdims=True)
     layer_out = jnp.sum(shares[:, :, None] * out_float, axis=1).astype(jnp.bfloat16)
     gram_part = jnp.einsum("tjd,tkd->tjk", out_float, out_float) / math.sqrt(full_width)
-    gram = lax.psum(gram_part, "half")
+    gram = take_quarters_here(gram_part)
     off_diag = 1.0 - jnp.eye(top_count, dtype=jnp.float32)
     coeffs = orth_weight * gram * off_diag
     grad_out = pad_mask.astype(jnp.float32)[:, None, None] * (

time: 344 us -> 343 us (level)
  blocking collectives: 178 us -> 166 us
  waiting for transfers between devices: 87.1 us -> 93.2 us
  starting transfers between devices: 37.2 us -> 42.5 us
    psum x1 -> x0, blocking collectives: 11.8 us -> none  [shards(): gram = lax.psum(gram_part, 'half')]
    ppermute x0 -> x2, waiting for transfers between devices: none -> 6.37 us  [perform_slot(): ppermute(main, axis_name=net_axis, perm=list(map(lambda no: (no, no ^ par...]
    ppermute x0 -> x2, starting transfers between devices: none -> 5.01 us  [perform_slot(): ppermute(main, axis_name=net_axis, perm=list(map(lambda no: (no, no ^ par...]
  transfers between devices with their start and end apart: 4 -> 6, of which waited for: 4 -> 6; matrix products, arithmetic and copies ran while one was open for 0% -> 0% of each run, Pallas kernels for 0% -> 0%
where the time goes in v1:
time: 343 us; the launch traced here: 342 us
  blocking collectives  166 us (48%)
  waiting for transfers between devices  93.2 us (27%)
  starting transfers between devices  42.5 us (12%)
  between operations  14.3 us (4%)
  local copies, waits for them, and re-layouts  13.8 us (4%)
  matrix products  9.93 us (3%)
    all_to_all x2, blocking collectives, to_experts(): lax.all_to_all(buckets, 'expert', split_axis=0, concat_axis=0, tiled=True)  145 us
    all_to_all x2, waiting for transfers between devices, to_homes(): lax.all_to_all(summed, 'expert', split_axis=0, concat_axis=0, tiled=True)  44.1 us
    reduce_scatter x2, waiting for transfers between devices, to_homes(): lax.psum_scatter(partial_value.astype(jnp.bfloat16), 'half', scatter_dime...  42.7 us
    all_to_all x2, starting transfers between devices, to_homes(): lax.all_to_all(summed, 'expert', split_axis=0, concat_axis=0, tiled=True)  37.4 us
    all_gather x2, blocking collectives, to_experts(): whole = lax.all_gather(items, 'half', axis=1, tiled=True)  21.1 us
  transfers between devices with their start and end apart: 6, of which 6 were waited for; matrix products, arithmetic and copies ran while one was open for 0% of the time, Pallas kernels for 0%

profile of v1, /device:TPU:1, one launch (start us, length us, event | category | flops | bytes accessed | tf_op | source)
XLA Modules:
  0.0 341.9 jit_solution(7083271647533160061)
XLA Ops:
  7.2 0.9 copy.17
  8.9 10.4 %all_gather.6 = bf16[16,2048]{1,0:T(8,128)(2,1)S(1)} all-gather(bf16[16,512]{1,0:T(8,128)(2,1)} %param.10), channel_id=1, replica_groups=mesh['expert'=128,'half'=4] {'half'}, dimensions={1}, use_global_device_ids=true | all-gather | bytes 81920 | tf_op jit(solution)/shard_map/all_gather | solution.py:49
  19.7 1.5 all_to_all.32
  21.2 77.1 %all_to_all.48 = bf16[128,2,2048]{2,1,0:T(2,128)(2,1)} all-to-all(bf16[128,2,2048]{2,1,0:T(2,128)(2,1)} %all_to_all.32), channel_id=1, replica_groups=mesh['expert'=128,'half'=4] {'expert'}, dimensions={0} | all-to-all | bytes 2097152 | tf_op jit(solution)/shard_map/all_to_all | solution.py:51
  98.3 1.5 all_to_all.34
  99.8 2.2 fusion.9
  102.0 0.7 fusion.5
  102.7 1.7 convolution_convert_fusion.1
  104.5 21.8 %reduce-scatter.3.cloned.1.call-done = bf16[256,512]{1,0:T(8,128)(2,1)} async-done(((bf16[256,2048]{1,0:T(8,128)(2,1)}), bf16[256,512]{1,0:T(8,128)(2,1)}) %reduce-scatter.3.cloned.1.call-update) | async-done | bytes 262160 | tf_op jit(solution)/shard_map/reduce_scatter | solution.py:55
  126.3 1.7 all_to_all.35
  128.1 18.7 %all-to-all-start.1 = ((bf16[128,2,512]{2,1,0:T(2,128)(2,1)}), bf16[128,2,512]{2,1,0:T(2,128)(2,1)S(1)}, u32[]{:S(2)}, u32[]{:S(2)}) async-start(bf16[128,2,512]{2,1,0:T(2,128)(2,1)} %all_to_all.35), calls=%async_computation.2 | async-start | bytes 524288 | tf_op jit(solution)/shard_map/all_to_all | solution.py:58
  146.9 22.4 %all-to-all-done.1 = bf16[128,2,512]{2,1,0:T(2,128)(2,1)S(1)} async-done(((bf16[128,2,512]{2,1,0:T(2,128)(2,1)}), bf16[128,2,512]{2,1,0:T(2,128)(2,1)S(1)}, u32[]{:S(2)}, u32[]{:S(2)}) %all-to-all-start.1) | async-done | bytes 262176 | tf_op jit(solution)/shard_map/all_to_all | solution.py:58
  169.4 0.8 gather_fusion
  170.5 1.9 collective-permute-start
  172.4 3.1 collective-permute-done
  175.5 3.1 collective-permute-start.1
  178.7 3.3 collective-permute-done.1
  182.3 10.8 %all_gather.7 = bf16[128,2048]{1,0:T(8,128)(2,1)S(1)} all-gather(bf16[128,512]{1,0:T(8,128)(2,1)S(1)} %fusion.13), channel_id=1, replica_groups=mesh['expert'=128,'half'=4] {'half'}, dimensions={1}, use_global_device_ids=true | all-gather | bytes 655360 | tf_op jit(solution)/shard_map/all_gather | solution.py:49
  193.1 1.1 convolution_convert_fusion
  194.2 1.5 all_to_all.38
  195.7 67.7 %all_to_all.49 = bf16[128,2,2048]{2,1,0:T(2,128)(2,1)} all-to-all(bf16[128,2,2048]{2,1,0:T(2,128)(2,1)} %all_to_all.38), channel_id=1, replica_groups=mesh['expert'=128,'half'=4] {'expert'}, dimensions={0} | all-to-all | bytes 2097152 | tf_op jit(solution)/shard_map/all_to_all | solution.py:51
  263.4 1.5 all_to_all.40
  264.9 0.7 fusion.1
  266.3 0.8 fusion.7
  267.7 1.8 fusion
  269.5 20.9 %reduce-scatter.5.cloned.1.call-done = bf16[256,512]{1,0:T(8,128)(2,1)} async-done(((bf16[256,2048]{1,0:T(8,128)(2,1)}), bf16[256,512]{1,0:T(8,128)(2,1)}) %reduce-scatter.5.cloned.1.call-update) | async-done | bytes 262160 | tf_op jit(solution)/shard_map/reduce_scatter | solution.py:55
  290.4 1.7 all_to_all.41
  292.1 18.7 %all-to-all-start.3 = ((bf16[128,2,512]{2,1,0:T(2,128)(2,1)}), bf16[128,2,512]{2,1,0:T(2,128)(2,1)S(1)}, u32[]{:S(2)}, u32[]{:S(2)}) async-start(bf16[128,2,512]{2,1,0:T(2,128)(2,1)} %all_to_all.41), calls=%async_computation.5 | async-start | bytes 524288 | tf_op jit(solution)/shard_map/all_to_all | solution.py:58
  310.8 0.8 multiply_reduce_fusion
  311.6 21.7 %all-to-all-done.3 = bf16[128,2,512]{2,1,0:T(2,128)(2,1)S(1)} async-done(((bf16[128,2,512]{2,1,0:T(2,128)(2,1)}), bf16[128,2,512]{2,1,0:T(2,128)(2,1)S(1)}, u32[]{:S(2)}, u32[]{:S(2)}) %all-to-all-start.3) | async-done | bytes 262176 | tf_op jit(solution)/shard_map/all_to_all | solution.py:58
  333.4 0.8 gather_fusion.1
  334.3 0.7 bitcast_reduce_fusion
  (42 shorter events, 3.5 us)
Async XLA Ops:
  7.2 95.6 %copy-start = (bf16[1,384,2048]{2,1,0:T(8,128)(2,1)S(1)}, bf16[1,384,2048]{2,1,0:T(8,128)(2,1)}, u32[]{:S(2)}) copy-start(bf16[1,384,2048]{2,1,0:T(8,128)(2,1)} %param.17) | copy-start | bytes 4718596
  7.2 119.1 %reduce-scatter.3.cloned.1.call-start = ((), (), s32[]{:S(2)}) async-start(), calls=%async_computation.6 | async-start | bytes 1310720 | tf_op jit(solution)/shard_map/reduce_scatter | solution.py:55
  99.7 2.2 copy-start.2
  104.4 42.4 %copy-start.5 = (f32[16,8]{0,1:T(8,128)S(1)}, f32[16,8]{0,1:T(8,128)}, u32[]{:S(2)}) copy-start(f32[16,8]{0,1:T(8,128)} %param.13) | copy-start | bytes 1540
  104.5 74.2 %copy-start.7 = (s32[16]{0:T(128)S(1)}, s32[16]{0:T(128)}, u32[]{:S(2)}) copy-start(s32[16]{0:T(128)} %param.14) | copy-start | bytes 196
  104.5 74.3 %copy-start.4 = (bf16[16,512]{1,0:T(8,128)(2,1)S(1)}, bf16[16,512]{1,0:T(8,128)(2,1)}, u32[]{:S(2)}) copy-start(bf16[16,512]{1,0:T(8,128)(2,1)} %param.11) | copy-start | bytes 49156
  128.1 41.2 %all-to-all-start.1 = ((bf16[128,2,512]{2,1,0:T(2,128)(2,1)}), bf16[128,2,512]{2,1,0:T(2,128)(2,1)S(1)}, u32[]{:S(2)}, u32[]{:S(2)}) async-start(bf16[128,2,512]{2,1,0:T(2,128)(2,1)} %all_to_all.35), calls=%async_computation.2 | async-start | bytes 524288 | tf_op jit(solution)/shard_map/all_to_all | solution.py:58
  146.8 143.6 %reduce-scatter.5.cloned.1.call-start = ((), (), s32[]{:S(2)}) async-start(), calls=%async_computation.7 | async-start | bytes 1310720 | tf_op jit(solution)/shard_map/reduce_scatter | solution.py:55
  146.9 22.4 %copy-start.6 = (s32[128]{0:T(128)}, s32[128]{0:T(128)S(1)}, u32[]{:S(2)}) copy-start(s32[128]{0:T(128)S(1)} %get-tuple-element.4) | copy-start | bytes 1540
  170.5 5.0 %collective-permute-start = (f32[16,8,8]{2,1,0:T(8,128)S(1)}, f32[16,8,8]{2,1,0:T(8,128)S(1)}, u32[]{:S(2)}, u32[]{:S(2)}) collective-permute-start(f32[16,8,8]{2,1,0:T(8,128)S(1)} %convolution_multiply_fusion), channel_id=1, source_target_pairs={{0,1},{1,0},{2,3},{3,2},{4,5},{5,4},{6,7},{7,6},{8,9},{9,8},{10,11... | collective-permute-start | bytes 12296 | tf_op jit(solution)/shard_map/ppermute | solution.py:20
  175.5 6.5 %collective-permute-start.1 = (f32[16,8,8]{2,1,0:T(8,128)S(1)}, f32[16,8,8]{2,1,0:T(8,128)S(1)}, u32[]{:S(2)}, u32[]{:S(2)}) collective-permute-start(f32[16,8,8]{2,1,0:T(8,128)S(1)} %add.43), channel_id=1, source_target_pairs={{0,2},{1,3},{2,0},{3,1},{4,6},{5,7},{6,4},{7,5},{8,10},{9,11},{10,... | collective-permute-start | bytes 12296 | tf_op jit(solution)/shard_map/ppermute | solution.py:20
  264.9 1.4 copy-start.1
  266.3 1.4 copy-start.3
  292.1 41.2 %all-to-all-start.3 = ((bf16[128,2,512]{2,1,0:T(2,128)(2,1)}), bf16[128,2,512]{2,1,0:T(2,128)(2,1)S(1)}, u32[]{:S(2)}, u32[]{:S(2)}) async-start(bf16[128,2,512]{2,1,0:T(2,128)(2,1)} %all_to_all.41), calls=%async_computation.5 | async-start | bytes 524288 | tf_op jit(solution)/shard_map/all_to_all | solution.py:58
Sparse Core Ops, SparseCore 0:
  104.6 21.6 reduce-scatter.2
  269.6 20.7 reduce-scatter.4
